TPU v7x, 256 devices: a whole 4x4x8 slice. The times are simulated.
256 devices in a mesh: tensor: 64 (over y, z, core), contract: 4 (over x).
Axes of the slice: x: 4, y: 4, z: 8, core: 2. Of those that a mesh axis runs over, the one named last changes fastest.
Arguments:
- amplitudes: float32 [256, 128, 128], P('tensor', 'contract'), may hold values from -6 to 6
- ladder_ints: float32 [128, 128, 16384], P('contract', None, 'tensor'), may hold values from -0.046875 to 0.046875
- cycle_ints: float32 [16, 128, 16, 128], P(None, None, None, 'contract'), may hold values from -0.125 to 0.125
- occ_energy: float32 [16], replicated, may hold values from -2 to -0.5
- virt_energy: float32 [128], replicated, may hold values from 0.5 to 3
Outputs:
- update: float32 [256, 128, 128], P(('tensor', 'contract'))
All inputs are finite; a program needn't handle non-finite values.
Results may differ from a plain program's by a relative error of at most 0.00007.
Values sent between devices are 32-bit elements; how exact they have to be, the bound alone decides.
A program may use at most 64 MiB of HBM per device.

v0:
```python
import jax
import jax.numpy as jnp
from jax import lax
from jax.sharding import PartitionSpec as P


def body(amplitudes, ladder_ints, cycle_ints, occ_energy, virt_energy):
    whole = lax.all_gather(amplitudes, "tensor", axis=0, tiled=True)
    pairs_all = whole.shape[0]
    c_local = whole.shape[1]
    virt = whole.shape[2]
    columns = ladder_ints.shape[2]
    nocc = cycle_ints.shape[0]
    ladder = jnp.dot(
        whole.reshape(pairs_all, c_local * virt),
        ladder_ints.reshape(c_local * virt, columns),
        precision=lax.Precision.HIGHEST,
        preferred_element_type=jnp.float32,
    )
    first_col = lax.axis_index("tensor") * columns
    needed = min(virt, (columns + virt - 1) // virt + 1)
    a_start = jnp.clip(first_col // virt, 0, virt - needed)
    chosen = lax.dynamic_slice_in_dim(cycle_ints, a_start, needed, 1)
    cycle_rows = jnp.einsum(
        "iakc,kjcb->ijab",
        chosen,
        whole.reshape(nocc, nocc, c_local, virt),
        precision=lax.Precision.HIGHEST,
    ).reshape(pairs_all, needed * virt)
    offset = first_col - a_start * virt
    cycle = lax.dynamic_slice_in_dim(cycle_rows, offset, columns, 1)
    partial_value = ladder + cycle
    owned = lax.all_to_all(partial_value, "tensor", split_axis=0, concat_axis=1, tiled=True)
    summed = lax.psum_scatter(owned, "contract", scatter_dimension=0, tiled=True)
    rows_here = summed.shape[0]
    first_row = lax.axis_index(("tensor", "contract")) * rows_here
    pair_ids = first_row + jnp.arange(rows_here, dtype=jnp.int32)
    occ_ids = jnp.arange(nocc, dtype=jnp.int32)
    pick_first = (occ_ids[None, :] == (pair_ids // nocc)[:, None]).astype(jnp.float32)
    pick_second = (occ_ids[None, :] == (pair_ids % nocc)[:, None]).astype(jnp.float32)
    occ_pair = jnp.sum(pick_first * occ_energy[None, :], axis=1) + jnp.sum(
        pick_second * occ_energy[None, :], axis=1
    )
    denom = virt_energy[None, :, None] + virt_energy[None, None, :] - occ_pair[:, None, None]
    return summed.reshape(rows_here, virt, virt) / denom


def solution(mesh):
    in_specs = (
        P("tensor", "contract", None),
        P("contract", None, "tensor"),
        P(None, None, None, "contract"),
        P(),
        P(),
    )
    out_specs = P(("tensor", "contract"), None, None)
    return jax.shard_map(body, mesh=mesh, in_specs=in_specs, out_specs=out_specs, check_vma=False)
```

profile of v0, /device:TPU:1, one launch (start us, length us, event | category | flops | bytes accessed | tf_op | source)
XLA Modules:
  0.0 181.5 jit_solution(6829998206768863437)
XLA Ops:
  6.5 0.0 all-gather.2.cloned.1.call-start
  6.5 0.7 all-gather.2.cloned.1.call-update
  7.3 0.0 all-reduce.3.cloned.1.call-start
  7.3 5.3 %constant_dynamic-slice_fusion.1 = f32[16,3,16,32]{1,3,2,0:T(8,128)} fusion(f32[16,128,16,32]{1,3,2,0:T(8,128)} %param.7, s32[]{:T(128)S(6)} %min.4), kind=kLoop, calls=%fused_computation.16 | loop fusion | bytes 196612 | tf_op jit(solution)/shard_map/dynamic_slice | solution.py:23
  12.6 3.4 %copy.23 = f32[16,3,16,32]{3,0,2,1:T(8,128)S(1)} copy(f32[16,3,16,32]{1,3,2,0:T(8,128)} %constant_dynamic-slice_fusion.1) | data formatting | bytes 196608
  16.0 77.4 %all-gather.2.cloned.1.call-done = f32[256,32,128]{2,1,0:T(8,128)} async-done(((f32[4,32,128]{2,1,0:T(8,128)}), f32[256,32,128]{2,1,0:T(8,128)}) %all-gather.2.cloned.1.call-update) | async-done | bytes 4194320 | tf_op jit(solution)/shard_map/all_gather | solution.py:8
  93.4 0.0 copy-start
  93.4 5.7 %fusion.5 = f32[16,16,3,128]{3,0,1,2:T(8,128)S(1)} fusion(f32[16,16,32,128]{3,2,1,0:T(8,128)} %bitcast.34, f32[16,3,16,32]{3,0,2,1:T(8,128)S(1)} %copy.23), kind=kOutput, calls=%fused_computation.5 | convolution fusion | flops 603979776 | bytes 4685824 | tf_op jit(solution)/shard_map/iakc,kjcb->ijab/dot_general | solution.py:24
  99.1 0.3 copy.20
  99.4 0.0 copy-done
  99.4 0.0 copy-start.3
  99.4 0.0 copy-start.2
  99.5 0.0 copy-start.1
  99.5 13.1 %fusion.11 = f32[256,256]{1,0:T(8,128)S(1)} fusion(f32[32,128,256]{2,1,0:T(8,128)} %param.6, f32[256,32,128]{2,1,0:T(8,128)S(1)} %copy-done, f32[256,384]{1,0:T(8,128)S(1)} %bitcast.36, s32[]{:T(128)S(6)} %select_n.21), kind=kOutput, calls=%fused_computation.7 | convolution fusion | flops 3221291008 | bytes 8912900 | tf_op jit(solution)/shard_map/dot_general | solution.py:14
  112.6 0.1 all_to_all.14
  112.7 18.2 %all_to_all.19 = f32[64,4,256]{2,1,0:T(4,128)} all-to-all(f32[64,4,256]{2,1,0:T(4,128)S(1)} %all_to_all.14), channel_id=1, replica_groups=mesh['tensor'=64,'contract'=4] {'tensor'}, dimensions={0} | all-to-all | bytes 524288 | tf_op jit(solution)/shard_map/all_to_all | solution.py:33
  130.8 0.0 all-reduce.3.cloned.1.call-update
  130.9 0.0 copy-done.3
  130.9 0.6 dynamic-slice
  131.5 0.0 copy-done.2
  131.5 0.7 fusion.16
  133.5 38.7 %all-reduce.3.cloned.1.call-done = f32[4,16384]{1,0:T(4,128)} async-done(((f32[4,16384]{1,0:T(4,128)}), f32[4,16384]{1,0:T(4,128)}) %all-reduce.3.cloned.1.call-update) | async-done | bytes 262160
  172.2 1.7 constant_dynamic-slice_fusion
  173.9 0.0 copy-done.1
  173.9 0.7 subtract_divide_fusion
  (1 shorter events, 0.0 us)
Async XLA Ops:
  6.5 86.9 %all-gather.2.cloned.1.call-start = ((), (), s32[]{:S(2)}) async-start(), calls=%async_computation.1 | async-start | bytes 4259840 | tf_op jit(solution)/shard_map/all_gather | solution.py:8
  7.3 165.0 %all-reduce.3.cloned.1.call-start = ((), (), s32[]{:S(2)}) async-start(), calls=%async_computation.2 | async-start | bytes 524288
  93.4 6.0 %copy-start = (f32[256,32,128]{2,1,0:T(8,128)S(1)}, f32[256,32,128]{2,1,0:T(8,128)}, u32[]{:S(2)}) copy-start(f32[256,32,128]{2,1,0:T(8,128)} %all-gather.2.cloned.1.call-done) | copy-start | bytes 12582916
  99.4 31.4 %copy-start.3 = (u32[256]{0:T(256)S(1)}, u32[256]{0:T(256)}, u32[]{:S(2)}) copy-start(u32[256]{0:T(256)} %constant.77) | copy-start | bytes 3076
  99.4 32.0 %copy-start.2 = (f32[16]{0:T(128)S(1)}, f32[16]{0:T(128)}, u32[]{:S(2)}) copy-start(f32[16]{0:T(128)} %param.8) | copy-start | bytes 196
  99.5 74.4 %copy-start.1 = (f32[128]{0:T(128)S(1)}, f32[128]{0:T(128)}, u32[]{:S(2)}) copy-start(f32[128]{0:T(128)} %param.9) | copy-start | bytes 1540
Sparse Core Ops, SparseCore 0:
  10.1 83.2 all-gather.1
  131.0 41.2 all-reduce.2
where the time goes:
time: 183 us; the launch traced here: 181 us
  waiting for transfers between devices  117 us (64%)
  matrix products  18.8 us (10%)
  blocking collectives  18.2 us (10%)
  between operations  14.9 us (8%)
  local copies, waits for them, and re-layouts  11.3 us (6%)
    all_gather x1, waiting for transfers between devices, body(): whole = lax.all_gather(amplitudes, 'tensor', axis=0, tiled=True)  77.4 us
    unnamed x3, waiting for transfers between devices  39.5 us
    all_to_all x1, blocking collectives, body(): lax.all_to_all(partial_value, 'tensor', split_axis=0, concat_axis=1, tile...  18.2 us
    dot_general x1, matrix products, body(): jnp.dot(whole.reshape(pairs_all, c_local * virt), ladder_ints.reshape(c_l...  13.1 us
    unnamed x12, local copies, waits for them, and re-layouts  5.68 us
    dot_general x1, matrix products, body(): jnp.einsum('iakc,kjcb->ijab', chosen, whole.reshape(nocc, nocc, c_local,...  5.65 us
    dynamic_slice x1, local copies, waits for them, and re-layouts, body(): chosen = lax.dynamic_slice_in_dim(cycle_ints, a_start, needed, 1)  5.31 us
  transfers between devices with their start and end apart: 2, of which 2 were waited for; matrix products, arithmetic and copies ran while one was open for 5% of the time, Pallas kernels for 0%

commit v1 on v0

v1 whole, which is shorter than its diff:
```python
import jax
import jax.numpy as jnp
from jax import lax
from jax.experimental import pallas as pl
from jax.experimental.pallas import tpu as pltpu
from jax.sharding import PartitionSpec as P

F32 = jnp.float32
BF16 = jnp.bfloat16
NY, NZ, NX = 4, 8, 4
PH = 4
CP = 4
ROWS = CP * 8
N_GATHER = 48


def split(v):
    hi = v.astype(BF16)
    lo = (v - hi.astype(F32)).astype(BF16)
    return hi, lo


def dot3(a, b):
    ahi, alo = a
    bhi, blo = b
    out = jnp.dot(ahi, bhi, preferred_element_type=F32)
    out += jnp.dot(ahi, blo, preferred_element_type=F32)
    out += jnp.dot(alo, bhi, preferred_element_type=F32)
    return out


def kernel(
    amps, ints, wts, out,
    raw, gat, vraw, vhi, vlo, wraw, sel, selt, wl_hi, wl_lo, lad, cyc, part, got1, got2, fin,
    lsem, ssem, rsem, asend, arecv,
):
    t = lax.axis_index("tensor")
    x = lax.axis_index("contract")
    h = t % 2
    u = t // 2
    z = u % NZ
    y = u // NZ

    def dev(yy, zz, hh, xx):
        return ((yy * NZ + zz) * 2 + hh, xx)

    sib = dev(y, z, 1 - h, x)

    def ymod(v):
        return (v + NY) % NY

    def zmod(v):
        return (v + NZ) % NZ

    bar = pltpu.get_barrier_semaphore()

    def greet(d):
        pl.semaphore_signal(bar, inc=1, device_id=d, device_id_type=pl.DeviceIdType.MESH)

    greet(sib)
    for dx in range(1, NX):
        greet((t, (x + dx) % NX))

    def greet_step(k, carry):
        uu = (u + k) % 32
        greet((uu * 2 + h, x))
        return carry

    lax.fori_loop(1, 32, greet_step, 0)

    wcopy = pltpu.make_async_copy(wts.at[:, :, pl.ds(h * 16, 16), :], wraw, lsem.at[0])
    acopy = pltpu.make_async_copy(
        amps.at[:, pl.ds(h * 16, 16), :], raw.at[pl.ds(h * 4, 4)], lsem.at[1]
    )
    acopy.start()
    own_cols = pl.multiple_of(h * 256, 256)
    sib_cols = pl.multiple_of((1 - h) * 256, 256)
    vcopies = [
        pltpu.make_async_copy(
            ints.at[pl.ds(h * 16 + q * CP, CP)],
            vraw.at[pl.ds(q * CP, CP), :, pl.ds(own_cols, 256)],
            lsem.at[2 + q],
        )
        for q in range(PH)
    ]
    wcopy.start()
    for c in vcopies:
        c.start()

    pl.semaphore_wait(bar, 31 + 1 + 3)

    sends = []

    def remote(n, src, dst, device):
        c = pltpu.make_async_remote_copy(
            src_ref=src, dst_ref=dst, send_sem=ssem.at[n], recv_sem=rsem.at[n],
            device_id=device, device_id_type=pl.DeviceIdType.MESH,
        )
        c.start()
        sends.append(c)

    def arrive(n, dst):
        pltpu.make_async_remote_copy(
            src_ref=dst, dst_ref=dst, send_sem=ssem.at[n], recv_sem=rsem.at[n],
            device_id=sib, device_id_type=pl.DeviceIdType.MESH,
        ).wait_recv()

    remote(0, amps.at[:, pl.ds((1 - h) * 16, 16), :], raw.at[pl.ds(h * 4, 4)], sib)
    for q in range(PH):
        remote(
            1 + q,
            ints.at[pl.ds((1 - h) * 16 + q * CP, CP)],
            vraw.at[pl.ds(q * CP, CP), :, pl.ds(own_cols, 256)],
            sib,
        )
    acopy.wait()
    arrive(0, raw.at[pl.ds((1 - h) * 4, 4)])

    for c in range(16):
        q, cc = c // CP, c % CP
        gat[q, y, z, cc * 8:(cc + 1) * 8, :] = raw[:, c, :]

    base = 8

    def yz_y(q):
        for dy in range(1, NY):
            remote(base + q * 12 + dy, gat.at[q, y, z], gat.at[q, y, z], dev(ymod(y + dy), z, h, x))

    def yz_y_arrive(q):
        for dy in range(1, NY):
            arrive(base + q * 12 + dy, gat.at[q, ymod(y - dy), z])

    def yz_z(q, s):
        n = base + q * 12 + 4 + 2 * (s - 1)
        ylo, yhi = ((0, 4), (0, 4)) if s < 4 else ((0, 2), (2, 2))
        a = gat.at[q, pl.ds(*ylo), zmod(z - (s - 1))]
        b = gat.at[q, pl.ds(*yhi), zmod(z + (s - 1))]
        remote(n, a, a, dev(y, zmod(z + 1), h, x))
        remote(n + 1, b, b, dev(y, zmod(z - 1), h, x))

    def yz_z_arrive(q, s):
        n = base + q * 12 + 4 + 2 * (s - 1)
        ylo, yhi = ((0, 4), (0, 4)) if s < 4 else ((0, 2), (2, 2))
        arrive(n, gat.at[q, pl.ds(*ylo), zmod(z - s)])
        arrive(n + 1, gat.at[q, pl.ds(*yhi), zmod(z + s)])

    def zy_z(q, s):
        n = base + q * 12 + 2 * (s - 1)
        rlo, rhi = ((0, ROWS), (0, ROWS)) if s < 4 else ((0, ROWS // 2), (ROWS // 2, ROWS // 2))
        a = gat.at[q, y, zmod(z - (s - 1)), pl.ds(*rlo)]
        b = gat.at[q, y, zmod(z + (s - 1)), pl.ds(*rhi)]
        remote(n, a, a, dev(y, zmod(z + 1), h, x))
        remote(n + 1, b, b, dev(y, zmod(z - 1), h, x))

    def zy_z_arrive(q, s):
        n = base + q * 12 + 2 * (s - 1)
        rlo, rhi = ((0, ROWS), (0, ROWS)) if s < 4 else ((0, ROWS // 2), (ROWS // 2, ROWS // 2))
        arrive(n, gat.at[q, y, zmod(z - s), pl.ds(*rlo)])
        arrive(n + 1, gat.at[q, y, zmod(z + s), pl.ds(*rhi)])

    def zy_y(q, s):
        n = base + q * 12 + 8 + 2 * (s - 1)
        zlo, zhi = ((0, 8), (0, 8)) if s < 2 else ((0, 4), (4, 4))
        a = gat.at[q, ymod(y - (s - 1)), pl.ds(*zlo)]
        b = gat.at[q, ymod(y + (s - 1)), pl.ds(*zhi)]
        remote(n, a, a, dev(ymod(y + 1), z, h, x))
        remote(n + 1, b, b, dev(ymod(y - 1), z, h, x))

    def zy_y_arrive(q, s):
        n = base + q * 12 + 8 + 2 * (s - 1)
        zlo, zhi = ((0, 8), (0, 8)) if s < 2 else ((0, 4), (4, 4))
        arrive(n, gat.at[q, ymod(y - s), pl.ds(*zlo)])
        arrive(n + 1, gat.at[q, ymod(y + s), pl.ds(*zhi)])

    def prepare_ints(q):
        vcopies[q].wait()
        arrive(1 + q, vraw.at[pl.ds(q * CP, CP), :, pl.ds(sib_cols, 256)])

        def step(c, carry):
            cc = q * CP + c
            hi, lo = split(vraw[cc])
            at = pl.multiple_of(cc * 128, 128)
            vhi[pl.ds(at, 128), :] = hi
            vlo[pl.ds(at, 128), :] = lo
            return carry

        lax.fori_loop(0, CP, step, 0)

    def prepare_weights():
        wcopy.wait()
        lane = lax.broadcasted_iota(jnp.int32, (256, 128), 1)

        def step(i, acc):
            w = wraw[i].reshape(256, 128)
            shift = (4 * i - 4 * u + 128) % 128
            return jnp.where(lane // 4 == i, pltpu.roll(w, shift, 1), acc)

        sel[...] = lax.fori_loop(0, 16, step, jnp.zeros((256, 128), F32))
        for half in range(2):
            block = jnp.concatenate(
                [sel[pl.ds(half * 8 + c, 16, stride=16), :] for c in range(8)], axis=0
            )
            selt[half] = block.T
            rows = jnp.concatenate(
                [selt.at[half][pl.ds(a, 16, stride=4), :] for a in range(4)], axis=0
            )
            hi, lo = split(rows)
            wl_hi[half] = hi
            wl_lo[half] = lo

    def ladder(q):
        a = jnp.concatenate(
            [gat[q, :, :, c * 8:(c + 1) * 8, :].reshape(256, 128) for c in range(CP)], axis=1
        )
        ahi, alo = split(a)
        for n in range(2):
            cols = slice(n * 256, (n + 1) * 256)
            rows = slice(q * CP * 128, (q + 1) * CP * 128)
            r = dot3((ahi, alo), (vhi[rows, cols], vlo[rows, cols]))
            for m in range(2):
                at = slice((2 * n + m) * 256, (2 * n + m + 1) * 256)
                val = r[:, m * 128:(m + 1) * 128]
                if q == 0:
                    lad[at, :] = val
                else:
                    lad[at, :] += val

    flat = gat.reshape(PH * 32 * ROWS, 128)

    def cycle(half):
        w = (wl_hi[half], wl_lo[half])

        def column(j):
            pieces = []
            for c in range(8):
                q, cc = half * 2 + c // CP, c % CP
                start = ((q * 32 + j // 8) * CP + cc) * 8 + j % 8
                pieces.append(flat[pl.ds(start, 16, stride=2 * ROWS), :])
            return jnp.concatenate(pieces, axis=0)

        for jp in range(8):
            b = jnp.concatenate([column(2 * jp), column(2 * jp + 1)], axis=1)
            r = dot3(w, split(b))
            for m in range(2):
                val = r[:, m * 128:(m + 1) * 128]
                at = slice((2 * jp + m) * 64, (2 * jp + m + 1) * 64)
                if half == 0:
                    cyc[at, :] = val
                else:
                    cyc[at, :] += val

    yz_y(0)
    zy_z(1, 1)
    yz_y(2)
    zy_z(3, 1)
    yz_y_arrive(0)
    yz_z(0, 1)
    zy_z_arrive(1, 1)
    zy_z(1, 2)
    zy_z_arrive(1, 2)
    zy_z(1, 3)
    yz_z_arrive(0, 1)
    yz_z(0, 2)
    zy_z_arrive(1, 3)
    zy_z(1, 4)
    zy_z_arrive(3, 1)
    zy_z(3, 2)
    yz_y_arrive(2)
    prepare_ints(0)
    zy_z_arrive(1, 4)
    zy_y(1, 1)
    yz_z_arrive(0, 2)
    yz_z(0, 3)
    zy_z_arrive(3, 2)
    zy_z(3, 3)
    yz_z(2, 1)
    prepare_weights()
    yz_z_arrive(0, 3)
    yz_z(0, 4)
    zy_z_arrive(3, 3)
    zy_z(3, 4)
    prepare_ints(1)
    yz_z_arrive(2, 1)
    yz_z(2, 2)
    zy_z_arrive(3, 4)
    zy_y(3, 1)
    zy_y_arrive(1, 1)
    zy_y(1, 2)
    yz_z_arrive(0, 4)
    ladder(0)
    prepare_ints(2)
    yz_z_arrive(2, 2)
    yz_z(2, 3)
    zy_y_arrive(1, 2)
    ladder(1)
    zy_y_arrive(3, 1)
    zy_y(3, 2)
    yz_z_arrive(2, 3)
    yz_z(2, 4)
    cycle(0)
    prepare_ints(3)
    zy_y_arrive(3, 2)
    ladder(3)
    yz_z_arrive(2, 4)
    ladder(2)
    cycle(1)

    def assemble(s):
        for jh in range(2):
            for a in range(4):
                l = lad[pl.ds(a * 256 + 8 * jh + s, 16, stride=16), :]
                c = cyc[pl.ds((jh * 8 + s) * 64 + a * 16, 16), :]
                part[pl.ds((s * 32 + jh * 16) * 4 + a, 16, stride=4), :] = l + c

    for s in range(8):
        assemble(s)

    n_core = 5
    sib_rows = pl.multiple_of((1 - h) * 512, 512)
    own_rows = pl.multiple_of(h * 512, 512)
    remote(n_core, part.at[pl.ds(sib_rows, 512), :], got1, sib)
    arrive(n_core, got1)
    got1[...] = got1[...] + part[pl.ds(own_rows, 512), :]

    n_x = base + 48
    for dx in range(1, NX):
        to = (x + dx) % NX
        remote(n_x + dx, got1.at[pl.ds(pl.multiple_of(to * 128, 128), 128), :], got2.at[dx - 1], (t, to))
    for dx in range(1, NX):
        arrive(n_x + dx, got2.at[dx - 1])
    mine = got1[pl.ds(pl.multiple_of(x * 128, 128), 128), :]
    fin[...] = mine + got2[0] + got2[1] + got2[2]

    def place(uu):
        return ((uu % 2) * 16 + uu // 2) * 4

    def a2a(k, to, frm):
        return pltpu.make_async_remote_copy(
            src_ref=fin.at[pl.ds(place(to), 4), :],
            dst_ref=out.at[pl.ds(frm * 4, 4), :],
            send_sem=asend.at[k], recv_sem=arecv.at[k],
            device_id=(to * 2 + h, x), device_id_type=pl.DeviceIdType.MESH,
        )

    def a2a_start(k, carry):
        a2a(k, (u + k) % 32, u).start()
        return carry

    lax.fori_loop(1, 32, a2a_start, 0)
    keep = pltpu.make_async_copy(fin.at[pl.ds(place(u), 4), :], out.at[pl.ds(u * 4, 4), :], lsem.at[6])
    keep.start()
    keep.wait()

    def a2a_wait(k, carry):
        a2a(k, (u + k) % 32, (u - k + 32) % 32).wait_recv()
        return carry

    lax.fori_loop(1, 32, a2a_wait, 0)

    def a2a_sent(k, carry):
        a2a(k, (u + k) % 32, u).wait_send()
        return carry

    lax.fori_loop(1, 32, a2a_sent, 0)
    for c in sends:
        c.wait_send()


def body(amplitudes, ladder_ints, cycle_ints, occ_energy, virt_energy):
    wts = jnp.transpose(cycle_ints, (0, 2, 3, 1))
    n_sem = 8 + 48 + 4
    summed = pl.pallas_call(
        kernel,
        out_shape=jax.ShapeDtypeStruct((128, 128), F32),
        in_specs=[pl.BlockSpec(memory_space=pl.ANY)] * 3,
        out_specs=pl.BlockSpec(memory_space=pltpu.VMEM),
        scratch_shapes=[
            pltpu.VMEM((8, 16, 128), F32),
            pltpu.VMEM((PH, NY, NZ, ROWS, 128), F32),
            pltpu.VMEM((16, 128, 512), F32),
            pltpu.VMEM((2048, 512), BF16),
            pltpu.VMEM((2048, 512), BF16),
            pltpu.VMEM((16, 16, 16, 128), F32),
            pltpu.VMEM((256, 128), F32),
            pltpu.VMEM((2, 128, 128), F32),
            pltpu.VMEM((2, 64, 128), BF16),
            pltpu.VMEM((2, 64, 128), BF16),
            pltpu.VMEM((1024, 128), F32),
            pltpu.VMEM((1024, 128), F32),
            pltpu.VMEM((1024, 128), F32),
            pltpu.VMEM((512, 128), F32),
            pltpu.VMEM((3, 128, 128), F32),
            pltpu.VMEM((128, 128), F32),
            pltpu.SemaphoreType.DMA((8,)),
            pltpu.SemaphoreType.DMA((n_sem,)),
            pltpu.SemaphoreType.DMA((n_sem,)),
            pltpu.SemaphoreType.DMA((32,)),
            pltpu.SemaphoreType.DMA((32,)),
        ],
        compiler_params=pltpu.CompilerParams(
            collective_id=0, has_side_effects=True, vmem_limit_bytes=48 * 1024 * 1024
        ),
        cost_estimate=pl.CostEstimate(flops=2_000_000_000, bytes_accessed=8_000_000, transcendentals=0),
        name="ladder_cycle",
    )(amplitudes, ladder_ints, wts)
    nocc = occ_energy.shape[0]
    pair = lax.axis_index("tensor") * NX + lax.axis_index("contract")
    occ_ids = jnp.arange(nocc, dtype=jnp.int32)
    occ_i = jnp.sum(jnp.where(occ_ids == pair // nocc, occ_energy, 0.0))
    occ_j = jnp.sum(jnp.where(occ_ids == pair % nocc, occ_energy, 0.0))
    denom = virt_energy[:, None] + virt_energy[None, :] - (occ_i + occ_j)
    return (summed / denom)[None]


def solution(mesh):
    in_specs = (
        P("tensor", "contract", None),
        P("contract", None, "tensor"),
        P(None, None, None, "contract"),
        P(),
        P(),
    )
    out_specs = P(("tensor", "contract"), None, None)
    return jax.shard_map(body, mesh=mesh, in_specs=in_specs, out_specs=out_specs, check_vma=False)
```

time: 183 us -> 67.8 us (0.37)
  waiting for transfers between devices: 117 us -> 0 us
  Pallas kernels: 0 us -> 61.1 us
  matrix products: 18.8 us -> 0 us
  blocking collectives: 18.2 us -> 0 us
  between operations: 14.9 us -> 1.37 us
  local copies, waits for them, and re-layouts: 11.3 us -> 3.03 us
    all_gather x1 -> x0, waiting for transfers between devices: 77.4 us -> none  [body(): whole = lax.all_gather(amplitudes, 'tensor', axis=0, tiled=True)]
    pallas_call x0 -> x1, Pallas kernels: none -> 61.1 us  [body(): pl.pallas_call(kernel, out_shape=jax.ShapeDtypeStruct((128, 128), F32), i...]
    unnamed x3 -> x0, waiting for transfers between devices: 39.5 us -> none
    dot_general x2 -> x0, matrix products: 18.8 us -> none  [the longest x1 13.1 us: body(): jnp.dot(whole.reshape(pairs_all, c_local * virt), ladder_ints.reshape(c_l...]
    all_to_all x1 -> x0, blocking collectives: 18.2 us -> none  [body(): lax.all_to_all(partial_value, 'tensor', split_axis=0, concat_axis=1, tile...]
    dynamic_slice x1 -> x0, local copies, waits for them, and re-layouts: 5.31 us -> none  [body(): chosen = lax.dynamic_slice_in_dim(cycle_ints, a_start, needed, 1)]
    unnamed x12 -> x6, local copies, waits for them, and re-layouts: 5.68 us -> 3.03 us
  transfers between devices with their start and end apart: 2 -> 0, of which waited for: 2 -> 0; matrix products, arithmetic and copies ran while one was open for 5% -> 0% of each run, Pallas kernels for 0% -> 0%
where the time goes in v1:
time: 67.8 us; the launch traced here: 67.6 us
  Pallas kernels  61.1 us (90%)
  local copies, waits for them, and re-layouts  3.03 us (4%)
  other arithmetic  2.07 us (3%)
  between operations  1.37 us (2%)
    pallas_call x1, Pallas kernels, body(): pl.pallas_call(kernel, out_shape=jax.ShapeDtypeStruct((128, 128), F32), i...  61.1 us
    unnamed x6, local copies, waits for them, and re-layouts  3.03 us

profile of v1, /device:TPU:1, one launch (start us, length us, event | category | flops | bytes accessed | tf_op | source)
XLA Modules:
  0.0 67.6 jit_solution(16522202892747021464)
XLA Ops:
  0.0 1.3 %fusion.1 = (f32[]{:T(128)}, f32[]{:T(128)}) fusion(f32[16]{0:T(128)} %param.8, s32[]{:T(128)S(6)} %select_n.20, s32[]{:T(128)S(6)} %select_n.18), kind=kLoop, calls=%fused_computation.4 | loop fusion | flops 94 | bytes 80 | tf_op jit(solution)/shard_map/reduce_sum | solution.py:410
  2.7 0.0 copy-start
  2.7 2.2 %copy-done = f32[32,128,256]{2,1,0:T(8,128)S(1)} copy-done((f32[32,128,256]{2,1,0:T(8,128)S(1)}, f32[32,128,256]{2,1,0:T(8,128)}, u32[]{:S(2)}) %copy-start) | copy-done | bytes 4194328
  4.9 0.0 copy-start.1
  4.9 0.8 %copy-done.1 = f32[4,32,128]{2,1,0:T(8,128)S(1)} copy-done((f32[4,32,128]{2,1,0:T(8,128)S(1)}, f32[4,32,128]{2,1,0:T(8,128)}, u32[]{:S(2)}) %copy-start.1) | copy-done | bytes 65560
  5.7 0.0 copy-start.2
  5.7 61.1 %ladder_cycle.1 = f32[128,128]{1,0:T(8,128)S(1)} custom-call(f32[4,32,128]{2,1,0:T(8,128)S(1)} %copy-done.1, f32[32,128,256]{2,1,0:T(8,128)S(1)} %copy-done, f32[16,16,32,128]{3,2,1,0:T(8,128)} %bitcast.3), custom_call_target="tpu_custom_call" | custom-call | flops 2000000000 | bytes 8000000 | tf_op jit(solution)/shard_map/ladder_cycle/pallas_call | solution.py:372
  66.9 0.0 copy-done.2
  66.9 0.7 %divide_bitcast_fusion = f32[1,128,128]{2,1,0:T(8,128)} fusion(f32[128,128]{1,0:T(8,128)S(1)} %ladder_cycle.1, f32[]{:T(128)S(6)} %add.29, f32[128]{0:T(128)S(1)} %copy-done.2), kind=kLoop, calls=%fused_computation | loop fusion | flops 49152 | bytes 131588 | tf_op jit(solution)/shard_map/broadcast_in_dim | solution.py:412
Async XLA Ops:
  2.7 2.2 %copy-start = (f32[32,128,256]{2,1,0:T(8,128)S(1)}, f32[32,128,256]{2,1,0:T(8,128)}, u32[]{:S(2)}) copy-start(f32[32,128,256]{2,1,0:T(8,128)} %ints.1) | copy-start | bytes 12582916
  4.9 0.8 %copy-start.1 = (f32[4,32,128]{2,1,0:T(8,128)S(1)}, f32[4,32,128]{2,1,0:T(8,128)}, u32[]{:S(2)}) copy-start(f32[4,32,128]{2,1,0:T(8,128)} %amps.1) | copy-start | bytes 196612
  5.7 61.2 %copy-start.2 = (f32[128]{0:T(128)S(1)}, f32[128]{0:T(128)}, u32[]{:S(2)}) copy-start(f32[128]{0:T(128)} %param.9) | copy-start | bytes 1540

commit v2 on v1

v2 whole, which is shorter than its diff:
```python
import jax
import jax.numpy as jnp
from jax import lax
from jax.experimental import pallas as pl
from jax.experimental.pallas import tpu as pltpu
from jax.sharding import PartitionSpec as P

F32 = jnp.float32
BF16 = jnp.bfloat16
NY, NZ, NX = 4, 8, 4
PH = 4
CP = 4
PHASES = (("yz", 0, 4), ("zy", 4, 6), ("zy", 10, 6))
ORDER = (
    "C0", "A0", "B0", "v0", "C1", "A1", "B1", "w", "A2", "C2", "B2", "A3",
    "A4", "B3", "C3", "A5", "B4", "v1", "A6", "A7", "B5", "C4", "v2", "A8",
    "B6", "A9", "B7", "v3", "C5", "B8", "B9", "mC", "A10", "mA", "B10", "mB",
)


def split(v):
    hi = v.astype(BF16)
    lo = (v - hi.astype(F32)).astype(BF16)
    return hi, lo


def dot3(a, b):
    ahi, alo = a
    bhi, blo = b
    out = jnp.dot(ahi, bhi, preferred_element_type=F32)
    out += jnp.dot(ahi, blo, preferred_element_type=F32)
    out += jnp.dot(alo, bhi, preferred_element_type=F32)
    return out


def kernel(
    amps, ints, wts, occ_in, virt_in, out,
    raw, gat_c, gat_a, gat_b, vraw, vhi, vlo, wraw, sel, selt, wl_hi, wl_lo, lad, cyc, part, got1, got2, fin, land, occ, virt, den,
    lsem, ssem, rsem, asend, arecv,
):
    gats = (gat_c, gat_a, gat_b)
    t = lax.axis_index("tensor")
    x = lax.axis_index("contract")
    h = t % 2
    u = t // 2
    z = u % NZ
    y = u // NZ

    def dev(yy, zz, hh, xx):
        return ((yy * NZ + zz) * 2 + hh, xx)

    sib = dev(y, z, 1 - h, x)

    def ymod(v):
        return (v + NY) % NY

    def zmod(v):
        return (v + NZ) % NZ

    bar = pltpu.get_barrier_semaphore()

    def greet(d):
        pl.semaphore_signal(bar, inc=1, device_id=d, device_id_type=pl.DeviceIdType.MESH)

    greet(sib)
    for dx in range(1, NX):
        greet((t, (x + dx) % NX))

    for dy in range(1, NY):
        greet(dev(ymod(y + dy), z, h, x))
    for dz in (1, 2, -1, -2):
        greet(dev(y, zmod(z + dz), h, x))

    wcopy = pltpu.make_async_copy(wts.at[:, :, pl.ds(h * 16, 16), :], wraw, lsem.at[0])
    acopy = pltpu.make_async_copy(
        amps.at[:, pl.ds(h * 16, 16), :], raw.at[pl.ds(h * 4, 4)], lsem.at[1]
    )
    acopy.start()
    own_cols = pl.multiple_of(h * 256, 256)
    sib_cols = pl.multiple_of((1 - h) * 256, 256)
    vcopies = [
        pltpu.make_async_copy(
            ints.at[pl.ds(h * 16 + q * CP, CP)],
            vraw.at[pl.ds(q * CP, CP), :, pl.ds(own_cols, 256)],
            lsem.at[2 + q],
        )
        for q in range(PH)
    ]
    wcopy.start()
    ecopies = [
        pltpu.make_async_copy(occ_in, occ, lsem.at[7]),
        pltpu.make_async_copy(virt_in, virt, lsem.at[8]),
    ]
    for c in ecopies:
        c.start()
    for c in vcopies:
        c.start()

    pl.semaphore_wait(bar, 1 + 3 + 3 + 4)

    sends = []

    def remote(n, src, dst, device):
        c = pltpu.make_async_remote_copy(
            src_ref=src, dst_ref=dst, send_sem=ssem.at[n], recv_sem=rsem.at[n],
            device_id=device, device_id_type=pl.DeviceIdType.MESH,
        )
        c.start()
        sends.append(c)

    def arrive(n, dst):
        pltpu.make_async_remote_copy(
            src_ref=dst, dst_ref=dst, send_sem=ssem.at[n], recv_sem=rsem.at[n],
            device_id=sib, device_id_type=pl.DeviceIdType.MESH,
        ).wait_recv()

    remote(0, amps.at[:, pl.ds((1 - h) * 16, 16), :], raw.at[pl.ds(h * 4, 4)], sib)
    for q in range(PH):
        remote(
            1 + q,
            ints.at[pl.ds((1 - h) * 16 + q * CP, CP)],
            vraw.at[pl.ds(q * CP, CP), :, pl.ds(own_cols, 256)],
            sib,
        )
    acopy.wait()
    arrive(0, raw.at[pl.ds((1 - h) * 4, 4)])

    for gat, (_, c0, nc) in zip(gats, PHASES):
        for c in range(nc):
            gat[y, z, c * 8:(c + 1) * 8, :] = raw[:, c0 + c, :]

    ids = {}

    def sem(key):
        return ids.setdefault(key, 8 + len(ids))

    def at_z(d):
        return (z + d + NZ) % NZ

    def at_y(d):
        return (y + d + NY) % NY

    def yz(q, k):
        gat = gats[q]
        if k > 0:
            if k == 1:
                for dy in range(1, NY):
                    arrive(sem((q, "y", dy)), gat.at[at_y(-dy), z])
            else:
                lo, hi = ((0, 4), (0, 4)) if k < 5 else ((0, 2), (2, 2))
                arrive(sem((q, "z+", k)), gat.at[pl.ds(*lo), at_z(-(k - 1))])
                arrive(sem((q, "z-", k)), gat.at[pl.ds(*hi), at_z(k - 1)])
        if k == 0:
            for dy in range(1, NY):
                remote(sem((q, "y", dy)), gat.at[y, z], gat.at[y, z], dev(at_y(dy), z, h, x))
        elif k < 5:
            lo, hi = ((0, 4), (0, 4)) if k < 4 else ((0, 2), (2, 2))
            a = gat.at[pl.ds(*lo), at_z(-(k - 1))]
            b = gat.at[pl.ds(*hi), at_z(k - 1)]
            remote(sem((q, "z+", k + 1)), a, a, dev(y, at_z(1), h, x))
            remote(sem((q, "z-", k + 1)), b, b, dev(y, at_z(-1), h, x))

    def zy(q, k):
        gat = gats[q]
        rows = PHASES[q][2] * 8
        half = PHASES[q][2] // 2 * 8
        cut = {1: pl.ds(0, half), -1: pl.ds(half, rows - half)}

        def own_z(d):
            remote(sem((q, "z", d)), gat.at[y, z], gat.at[y, z], dev(y, at_z(d), h, x))

        def got_z(d):
            if abs(d) < 4:
                arrive(sem((q, "z", -d)), gat.at[y, at_z(d)])
            else:
                for sign in (1, -1):
                    arrive(sem((q, "z4", sign)), gat.at[y, at_z(4), cut[sign]])

        def forward_z(sign):
            b = gat.at[y, at_z(-2 * sign)]
            remote(sem((q, "z", 3 * sign)), b, b, dev(y, at_z(sign), h, x))
            c = gat.at[y, at_z(-2 * sign), cut[sign]]
            remote(sem((q, "z4", sign)), c, c, dev(y, at_z(2 * sign), h, x))

        def y1(d):
            for sign in (1, -1):
                b = gat.at[y, at_z(d)]
                remote(sem((q, "y1", d, sign)), b, b, dev(at_y(sign), z, h, x))

        def got_y1(d):
            for sign in (1, -1):
                arrive(sem((q, "y1", d, sign)), gat.at[at_y(-sign), at_z(d)])

        def y2(d, sign):
            b = gat.at[at_y(-sign), at_z(d)]
            remote(sem((q, "y2", d)), b, b, dev(at_y(sign), z, h, x))

        def got_y2(d):
            arrive(sem((q, "y2", d)), gat.at[at_y(2), at_z(d)])

        if k == 0:
            for d in (1, -1, 2, -2):
                own_z(d)
            y1(0)
        elif k == 1:
            got_z(1); got_z(-1)
            y1(1); y1(-1)
        elif k == 2:
            got_z(2); got_z(-2)
            forward_z(1); forward_z(-1)
            y1(2); y1(-2)
        elif k == 3:
            got_y1(0)
            y2(0, 1)
        elif k == 4:
            got_z(3); got_z(-3)
            y1(3); y1(-3)
        elif k == 5:
            got_y1(1); got_y1(-1)
            y2(1, 1); y2(-1, -1)
        elif k == 6:
            got_z(4)
            y1(4)
        elif k == 7:
            got_y1(2); got_y1(-2)
            y2(-2, 1); y2(2, -1)
        elif k == 8:
            got_y1(3); got_y1(-3)
            y2(3, 1); y2(-3, -1)
        elif k == 9:
            got_y1(4)
            y2(4, -1)
        elif k == 10:
            for d in (0, 1, -1, -2, 2, 3, -3, 4):
                got_y2(d)

    def prepare_ints(q):
        vcopies[q].wait()
        arrive(1 + q, vraw.at[pl.ds(q * CP, CP), :, pl.ds(sib_cols, 256)])

        def step(c, carry):
            cc = q * CP + c
            hi, lo = split(vraw[cc])
            at = pl.multiple_of(cc * 128, 128)
            vhi[pl.ds(at, 128), :] = hi
            vlo[pl.ds(at, 128), :] = lo
            return carry

        lax.fori_loop(0, CP, step, 0)

    def prepare_energies():
        for c in ecopies:
            c.wait()
        pair = t * NX + x
        who = lax.broadcasted_iota(jnp.int32, (1, 16), 1)
        o = occ[...]
        o = jnp.where(who == pair // 16, o, 0.0) + jnp.where(who == pair % 16, o, 0.0)
        v = jnp.broadcast_to(virt[...], (128, 128))
        den[...] = v.T + v - jnp.sum(o, axis=1, keepdims=True)

    def prepare_weights():
        wcopy.wait()
        lane = lax.broadcasted_iota(jnp.int32, (256, 128), 1)

        def step(i, acc):
            w = wraw[i].reshape(256, 128)
            shift = (4 * i - 4 * u + 128) % 128
            return jnp.where(lane // 4 == i, pltpu.roll(w, shift, 1), acc)

        sel[...] = lax.fori_loop(0, 16, step, jnp.zeros((256, 128), F32))
        for q, (_, c0, nc) in enumerate(PHASES):
            block = jnp.concatenate(
                [sel[pl.ds(c0 + c, 16, stride=16), :] for c in range(nc)], axis=0
            )
            block = jnp.concatenate([block, jnp.zeros((128 - nc * 16, 128), F32)], axis=0)
            selt[q] = block.T
            rows = jnp.concatenate(
                [selt.at[q][pl.ds(a, 16, stride=4), :] for a in range(4)], axis=0
            )
            hi, lo = split(rows)
            wl_hi[q] = hi
            wl_lo[q] = lo

    def ladder(q, first):
        gat = gats[q]
        _, c0, nc = PHASES[q]
        a = jnp.concatenate(
            [gat[:, :, c * 8:(c + 1) * 8, :].reshape(256, 128) for c in range(nc)], axis=1
        )
        ahi, alo = split(a)
        for n in range(2):
            cols = slice(n * 256, (n + 1) * 256)
            rows = slice(c0 * 128, (c0 + nc) * 128)
            r = dot3((ahi, alo), (vhi[rows, cols], vlo[rows, cols]))
            for m in range(2):
                at = slice((2 * n + m) * 256, (2 * n + m + 1) * 256)
                val = r[:, m * 128:(m + 1) * 128]
                if first:
                    lad[at, :] = val
                else:
                    lad[at, :] += val

    def cycle(q, first):
        _, c0, nc = PHASES[q]
        flat = gats[q].reshape(32 * nc * 8, 128)
        w = (wl_hi[q, :, 0:nc * 16], wl_lo[q, :, 0:nc * 16])

        def column(j):
            return jnp.concatenate(
                [
                    flat[pl.ds(((j // 8) * nc + c) * 8 + j % 8, 16, stride=2 * nc * 8), :]
                    for c in range(nc)
                ],
                axis=0,
            )

        for jp in range(8):
            b = jnp.concatenate([column(2 * jp), column(2 * jp + 1)], axis=1)
            r = dot3(w, split(b))
            for m in range(2):
                val = r[:, m * 128:(m + 1) * 128]
                at = slice((2 * jp + m) * 64, (2 * jp + m + 1) * 64)
                if first:
                    cyc[at, :] = val
                else:
                    cyc[at, :] += val

    first = True
    for step in ORDER:
        if step == "w":
            prepare_weights()
            prepare_energies()
        elif step[0] == "v":
            prepare_ints(int(step[1:]))
        elif step[0] == "m":
            q = "CAB".index(step[1])
            ladder(q, first)
            cycle(q, first)
            first = False
        else:
            q = "CAB".index(step[0])
            (yz if PHASES[q][0] == "yz" else zy)(q, int(step[1:]))

    def assemble(s):
        for jh in range(2):
            for a in range(4):
                l = lad[pl.ds(a * 256 + 8 * jh + s, 16, stride=16), :]
                c = cyc[pl.ds((jh * 8 + s) * 64 + a * 16, 16), :]
                part[pl.ds((s * 32 + jh * 16) * 4 + a, 16, stride=4), :] = l + c

    for s in range(8):
        assemble(s)

    n_core = 5
    sib_rows = pl.multiple_of((1 - h) * 512, 512)
    own_rows = pl.multiple_of(h * 512, 512)
    remote(n_core, part.at[pl.ds(sib_rows, 512), :], got1, sib)
    arrive(n_core, got1)
    got1[...] = got1[...] + part[pl.ds(own_rows, 512), :]

    n_x = 8 + len(ids)
    for dx in range(1, NX):
        to = (x + dx) % NX
        remote(n_x + dx, got1.at[pl.ds(pl.multiple_of(to * 128, 128), 128), :], got2.at[dx - 1], (t, to))
    for dx in range(1, NX):
        arrive(n_x + dx, got2.at[dx - 1])
    mine = got1[pl.ds(pl.multiple_of(x * 128, 128), 128), :]
    fin[...] = mine + got2[0] + got2[1] + got2[2]

    def place(uu):
        return ((uu % 2) * 16 + uu // 2) * 4

    def a2a(k, to, frm):
        return pltpu.make_async_remote_copy(
            src_ref=fin.at[pl.ds(place(to), 4), :],
            dst_ref=land.at[pl.ds(frm * 4, 4), :],
            send_sem=asend.at[k], recv_sem=arecv.at[k],
            device_id=(to * 2 + h, x), device_id_type=pl.DeviceIdType.MESH,
        )

    def a2a_start(k, carry):
        a2a(k, (u + k) % 32, u).start()
        return carry

    lax.fori_loop(1, 32, a2a_start, 0)
    keep = pltpu.make_async_copy(fin.at[pl.ds(place(u), 4), :], land.at[pl.ds(u * 4, 4), :], lsem.at[6])
    keep.start()
    keep.wait()

    def a2a_wait(k, carry):
        a2a(k, (u + k) % 32, (u - k + 32) % 32).wait_recv()
        return carry

    lax.fori_loop(1, 32, a2a_wait, 0)
    out[...] = land[...] / den[...]

    def a2a_sent(k, carry):
        a2a(k, (u + k) % 32, u).wait_send()
        return carry

    lax.fori_loop(1, 32, a2a_sent, 0)
    for c in sends:
        c.wait_send()


def body(amplitudes, ladder_ints, cycle_ints, occ_energy, virt_energy):
    wts = jnp.transpose(cycle_ints, (0, 2, 3, 1))
    n_sem = 120
    summed = pl.pallas_call(
        kernel,
        out_shape=jax.ShapeDtypeStruct((128, 128), F32),
        in_specs=[pl.BlockSpec(memory_space=pl.ANY)] * 5,
        out_specs=pl.BlockSpec(memory_space=pltpu.VMEM),
        scratch_shapes=[
            pltpu.VMEM((8, 16, 128), F32),
            *[pltpu.VMEM((NY, NZ, nc * 8, 128), F32) for _, _, nc in PHASES],
            pltpu.VMEM((16, 128, 512), F32),
            pltpu.VMEM((2048, 512), BF16),
            pltpu.VMEM((2048, 512), BF16),
            pltpu.VMEM((16, 16, 16, 128), F32),
            pltpu.VMEM((256, 128), F32),
            pltpu.VMEM((3, 128, 128), F32),
            pltpu.VMEM((3, 64, 128), BF16),
            pltpu.VMEM((3, 64, 128), BF16),
            pltpu.VMEM((1024, 128), F32),
            pltpu.VMEM((1024, 128), F32),
            pltpu.VMEM((1024, 128), F32),
            pltpu.VMEM((512, 128), F32),
            pltpu.VMEM((3, 128, 128), F32),
            pltpu.VMEM((128, 128), F32),
            pltpu.VMEM((128, 128), F32),
            pltpu.VMEM((1, 16), F32),
            pltpu.VMEM((1, 128), F32),
            pltpu.VMEM((128, 128), F32),
            pltpu.SemaphoreType.DMA((9,)),
            pltpu.SemaphoreType.DMA((n_sem,)),
            pltpu.SemaphoreType.DMA((n_sem,)),
            pltpu.SemaphoreType.DMA((32,)),
            pltpu.SemaphoreType.DMA((32,)),
        ],
        compiler_params=pltpu.CompilerParams(
            collective_id=0, has_side_effects=True, vmem_limit_bytes=60 * 1024 * 1024
        ),
        cost_estimate=pl.CostEstimate(flops=2_000_000_000, bytes_accessed=8_000_000, transcendentals=0),
        name="ladder_cycle",
    )(amplitudes, ladder_ints, wts, occ_energy.reshape(1, -1), virt_energy.reshape(1, -1))
    return summed[None]


def solution(mesh):
    in_specs = (
        P("tensor", "contract", None),
        P("contract", None, "tensor"),
        P(None, None, None, "contract"),
        P(),
        P(),
    )
    out_specs = P(("tensor", "contract"), None, None)
    return jax.shard_map(body, mesh=mesh, in_specs=in_specs, out_specs=out_specs, check_vma=False)
```

time: 67.8 us -> 52.1 us (0.77)
  Pallas kernels: 61.1 us -> 50.5 us
  other arithmetic: 2.07 us -> 0 us
  local copies, waits for them, and re-layouts: 3.03 us -> 1.47 us
  between operations: 1.37 us -> 0.01 us
    pallas_call x1, Pallas kernels: 61.1 us -> 50.5 us  [body(): pl.pallas_call(kernel, out_shape=jax.ShapeDtypeStruct((128, 128), F32), i...]
    unnamed x6 -> x1, local copies, waits for them, and re-layouts: 3.03 us -> 1.47 us
    reduce_sum x1 -> x0, other arithmetic: 1.34 us -> none  [body(): occ_j = jnp.sum(jnp.where(occ_ids == pair % nocc, occ_energy, 0.0))]
    broadcast_in_dim x1 -> x0, other arithmetic: 0.73 us -> none  [body(): return (summed / denom)[None]]
where the time goes in v2:
time: 52.1 us; the launch traced here: 52 us
  Pallas kernels  50.5 us (97%)
  local copies, waits for them, and re-layouts  1.47 us (3%)
    pallas_call x1, Pallas kernels, body(): pl.pallas_call(kernel, out_shape=jax.ShapeDtypeStruct((128, 128), F32), i...  50.5 us
    unnamed x1, local copies, waits for them, and re-layouts  1.47 us

profile of v2, /device:TPU:1, one launch (start us, length us, event | category | flops | bytes accessed | tf_op | source)
XLA Modules:
  0.0 52.0 jit_solution(14019155815459916837)
XLA Ops:
  0.0 50.5 %ladder_cycle.1 = f32[128,128]{1,0:T(8,128)} custom-call(f32[4,32,128]{2,1,0:T(8,128)} %amps.1, f32[32,128,256]{2,1,0:T(8,128)} %ints.1, f32[16,16,32,128]{3,2,1,0:T(8,128)} %bitcast.4, f32[1,16]{1,0:T(1,128)} %bitcast.6, f32[1,128]{1,0:T(1,128)} %bitcast.7), custom_call_target="tpu_custom_call" | custom-call | flops 2000000000 | bytes 8000000 | tf_op jit(solution)/shard_map/ladder_cycle/pallas_call | solution.py:409
  50.5 1.5 %copy.7 = f32[1,128,128]{2,1,0:T(8,128)} copy(f32[1,128,128]{2,1,0:T(8,128)} %bitcast.5) | data formatting | bytes 131072

commit v3 on v2

--- a/solution.py
+++ b/solution.py
@@ -10,11 +10,12 @@
 NY, NZ, NX = 4, 8, 4
 PH = 4
 CP = 4
-PHASES = (("yz", 0, 4), ("zy", 4, 6), ("zy", 10, 6))
+PHASES = (("yz", 0, 4), ("zy", 4, 7), ("zy", 11, 5))
 ORDER = (
-    "C0", "A0", "B0", "v0", "C1", "A1", "B1", "w", "A2", "C2", "B2", "A3",
-    "A4", "B3", "C3", "A5", "B4", "v1", "A6", "A7", "B5", "C4", "v2", "A8",
-    "B6", "A9", "B7", "v3", "C5", "B8", "B9", "mC", "A10", "mA", "B10", "mB",
+    "C0", "B0", "A0", "w", "B1", "B3", "C1", "A1", "B2", "A2", "B5", "C20",
+    "C21", "B4", "B6", "A4", "v0", "v3", "C30", "A6", "C31", "v1", "B7", "B8",
+    "B9", "C40", "A8", "A3", "v2", "A9", "C41", "A7", "A5", "Bt", "mB", "C5",
+    "mC", "At", "mA",
 )
 
 
@@ -140,25 +141,32 @@
     def at_y(d):
         return (y + d + NY) % NY
 
-    def yz(q, k):
+    def yz(q, k, pieces):
         gat = gats[q]
-        if k > 0:
-            if k == 1:
-                for dy in range(1, NY):
-                    arrive(sem((q, "y", dy)), gat.at[at_y(-dy), z])
-            else:
-                lo, hi = ((0, 4), (0, 4)) if k < 5 else ((0, 2), (2, 2))
-                arrive(sem((q, "z+", k)), gat.at[pl.ds(*lo), at_z(-(k - 1))])
-                arrive(sem((q, "z-", k)), gat.at[pl.ds(*hi), at_z(k - 1)])
+
+        def group(p, d):
+            return gat.at[pl.ds(2 * p, 2), at_z(d)]
+
+        def last(p, sign, step):
+            return step < 4 or (p == 0) == (sign == 1)
+
         if k == 0:
             for dy in range(1, NY):
                 remote(sem((q, "y", dy)), gat.at[y, z], gat.at[y, z], dev(at_y(dy), z, h, x))
-        elif k < 5:
-            lo, hi = ((0, 4), (0, 4)) if k < 4 else ((0, 2), (2, 2))
-            a = gat.at[pl.ds(*lo), at_z(-(k - 1))]
-            b = gat.at[pl.ds(*hi), at_z(k - 1)]
-            remote(sem((q, "z+", k + 1)), a, a, dev(y, at_z(1), h, x))
-            remote(sem((q, "z-", k + 1)), b, b, dev(y, at_z(-1), h, x))
+            return
+        if k == 1:
+            for dy in range(1, NY):
+                arrive(sem((q, "y", dy)), gat.at[at_y(-dy), z])
+        for p in pieces:
+            if k > 1:
+                for sign in (1, -1):
+                    if last(p, sign, k - 1):
+                        arrive(sem((q, "z", k - 1, sign, p)), group(p, -sign * (k - 1)))
+            if k < 5:
+                for sign in (1, -1):
+                    if last(p, sign, k):
+                        b = group(p, -sign * (k - 1))
+                        remote(sem((q, "z", k, sign, p)), b, b, dev(y, at_z(sign), h, x))
 
     def zy(q, k):
         gat = gats[q]
@@ -339,7 +347,10 @@
             first = False
         else:
             q = "CAB".index(step[0])
-            (yz if PHASES[q][0] == "yz" else zy)(q, int(step[1:]))
+            if PHASES[q][0] == "yz":
+                yz(q, int(step[1]), [int(p) for p in step[2:]] or [0, 1])
+            else:
+                zy(q, 10 if step[1] == "t" else int(step[1:]))
 
     def assemble(s):
         for jh in range(2):
@@ -408,7 +419,7 @@
     n_sem = 120
     summed = pl.pallas_call(
         kernel,
-        out_shape=jax.ShapeDtypeStruct((128, 128), F32),
+        out_shape=pltpu.VMEM((128, 128), F32),
         in_specs=[pl.BlockSpec(memory_space=pl.ANY)] * 5,
         out_specs=pl.BlockSpec(memory_space=pltpu.VMEM),
         scratch_shapes=[
@@ -439,7 +450,7 @@
             pltpu.SemaphoreType.DMA((32,)),
         ],
         compiler_params=pltpu.CompilerParams(
-            collective_id=0, has_side_effects=True, vmem_limit_bytes=60 * 1024 * 1024
+            collective_id=0, has_side_effects=True, vmem_limit_bytes=56 * 1024 * 1024
         ),
         cost_estimate=pl.CostEstimate(flops=2_000_000_000, bytes_accessed=8_000_000, transcendentals=0),
         name="ladder_cycle",

time: 52.1 us -> 46.2 us (0.89)
  Pallas kernels: 50.5 us -> 45.5 us
  local copies, waits for them, and re-layouts: 1.47 us -> 0.63 us
    pallas_call x1, Pallas kernels: 50.5 us -> 45.5 us  [body(): pl.pallas_call(kernel, out_shape=pltpu.VMEM((128, 128), F32), in_specs=[p...]
    unnamed x1, local copies, waits for them, and re-layouts: 1.47 us -> 0.63 us
where the time goes in v3:
time: 46.2 us; the launch traced here: 46.1 us
  Pallas kernels  45.5 us (98%)
  local copies, waits for them, and re-layouts  0.63 us (1%)
    pallas_call x1, Pallas kernels, body(): pl.pallas_call(kernel, out_shape=pltpu.VMEM((128, 128), F32), in_specs=[p...  45.5 us

profile of v3, /device:TPU:1, one launch (start us, length us, event | category | flops | bytes accessed | tf_op | source)
XLA Modules:
  0.0 46.1 jit_solution(13522686972188604881)
XLA Ops:
  0.0 45.5 %ladder_cycle.1 = f32[128,128]{1,0:T(8,128)S(1)} custom-call(f32[4,32,128]{2,1,0:T(8,128)} %amps.1, f32[32,128,256]{2,1,0:T(8,128)} %ints.1, f32[16,16,32,128]{3,2,1,0:T(8,128)} %bitcast.5, f32[1,16]{1,0:T(1,128)} %bitcast.6, f32[1,128]{1,0:T(1,128)} %bitcast.7), custom_call_target="tpu_custom_call" | custom-call | flops 2000000000 | bytes 8000000 | tf_op jit(solution)/shard_map/ladder_cycle/pallas_call | solution.py:420
  45.5 0.6 %copy.7 = f32[1,128,128]{2,1,0:T(8,128)} copy(f32[1,128,128]{2,1,0:T(8,128)S(1)} %bitcast.4) | data formatting | bytes 131072

commit v4 on v3

--- a/solution.py
+++ b/solution.py
@@ -370,7 +370,7 @@
     got1[...] = got1[...] + part[pl.ds(own_rows, 512), :]
 
     n_x = 8 + len(ids)
-    for dx in range(1, NX):
+    for dx in (2, 1, 3):
         to = (x + dx) % NX
         remote(n_x + dx, got1.at[pl.ds(pl.multiple_of(to * 128, 128), 128), :], got2.at[dx - 1], (t, to))
     for dx in range(1, NX):

time: 46.2 us -> 45.7 us (0.989)
  Pallas kernels: 45.5 us -> 45 us
    pallas_call x1, Pallas kernels: 45.5 us -> 45 us  [body(): pl.pallas_call(kernel, out_shape=pltpu.VMEM((128, 128), F32), in_specs=[p...]
where the time goes in v4:
time: 45.7 us; the launch traced here: 45.6 us
  Pallas kernels  45 us (98%)
  local copies, waits for them, and re-layouts  0.63 us (1%)
    pallas_call x1, Pallas kernels, body(): pl.pallas_call(kernel, out_shape=pltpu.VMEM((128, 128), F32), in_specs=[p...  45 us

profile of v4, /device:TPU:1, one launch (start us, length us, event | category | flops | bytes accessed | tf_op | source)
XLA Modules:
  0.0 45.6 jit_solution(15831131452721673352)
XLA Ops:
  0.0 45.0 %ladder_cycle.1 = f32[128,128]{1,0:T(8,128)S(1)} custom-call(f32[4,32,128]{2,1,0:T(8,128)} %amps.1, f32[32,128,256]{2,1,0:T(8,128)} %ints.1, f32[16,16,32,128]{3,2,1,0:T(8,128)} %bitcast.5, f32[1,16]{1,0:T(1,128)} %bitcast.6, f32[1,128]{1,0:T(1,128)} %bitcast.7), custom_call_target="tpu_custom_call" | custom-call | flops 2000000000 | bytes 8000000 | tf_op jit(solution)/shard_map/ladder_cycle/pallas_call | solution.py:420
  45.0 0.6 %copy.7 = f32[1,128,128]{2,1,0:T(8,128)} copy(f32[1,128,128]{2,1,0:T(8,128)S(1)} %bitcast.4) | data formatting | bytes 131072

commit v5 on v4

--- a/solution.py
+++ b/solution.py
@@ -385,7 +385,7 @@
         return pltpu.make_async_remote_copy(
             src_ref=fin.at[pl.ds(place(to), 4), :],
             dst_ref=land.at[pl.ds(frm * 4, 4), :],
-            send_sem=asend.at[k], recv_sem=arecv.at[k],
+            send_sem=asend.at[0], recv_sem=arecv.at[0],
             device_id=(to * 2 + h, x), device_id_type=pl.DeviceIdType.MESH,
         )
 
@@ -398,20 +398,19 @@
     keep.start()
     keep.wait()
 
-    def a2a_wait(k, carry):
-        a2a(k, (u + k) % 32, (u - k + 32) % 32).wait_recv()
-        return carry
-
-    lax.fori_loop(1, 32, a2a_wait, 0)
-    out[...] = land[...] / den[...]
-
-    def a2a_sent(k, carry):
-        a2a(k, (u + k) % 32, u).wait_send()
-        return carry
-
-    lax.fori_loop(1, 32, a2a_sent, 0)
     for c in sends:
         c.wait_send()
+
+    rest = pltpu.make_async_remote_copy(
+        src_ref=fin.at[pl.ds(0, 124), :],
+        dst_ref=land.at[pl.ds(0, 124), :],
+        send_sem=asend.at[0], recv_sem=arecv.at[0],
+        device_id=sib, device_id_type=pl.DeviceIdType.MESH,
+    )
+    rest.wait_recv()
+    out[...] = land[...] / den[...]
+
+    rest.wait_send()
 
 
 def body(amplitudes, ladder_ints, cycle_ints, occ_energy, virt_energy):
@@ -446,8 +445,8 @@
             pltpu.SemaphoreType.DMA((9,)),
             pltpu.SemaphoreType.DMA((n_sem,)),
             pltpu.SemaphoreType.DMA((n_sem,)),
-            pltpu.SemaphoreType.DMA((32,)),
-            pltpu.SemaphoreType.DMA((32,)),
+            pltpu.SemaphoreType.DMA((1,)),
+            pltpu.SemaphoreType.DMA((1,)),
         ],
         compiler_params=pltpu.CompilerParams(
             collective_id=0, has_side_effects=True, vmem_limit_bytes=56 * 1024 * 1024

time: 45.7 us -> 44.7 us (0.978)
  Pallas kernels: 45 us -> 44 us
    pallas_call x1, Pallas kernels: 45 us -> 44 us  [body(): pl.pallas_call(kernel, out_shape=pltpu.VMEM((128, 128), F32), in_specs=[p...]
where the time goes in v5:
time: 44.7 us
  Pallas kernels  44 us (98%)
  local copies, waits for them, and re-layouts  0.63 us (1%)
    pallas_call x1, Pallas kernels, body(): pl.pallas_call(kernel, out_shape=pltpu.VMEM((128, 128), F32), in_specs=[p...  44 us

profile of v5, /device:TPU:1, one launch (start us, length us, event | category | flops | bytes accessed | tf_op | source)
XLA Modules:
  0.0 44.7 jit_solution(2723692937349703619)
XLA Ops:
  0.0 44.0 %ladder_cycle.1 = f32[128,128]{1,0:T(8,128)S(1)} custom-call(f32[4,32,128]{2,1,0:T(8,128)} %amps.1, f32[32,128,256]{2,1,0:T(8,128)} %ints.1, f32[16,16,32,128]{3,2,1,0:T(8,128)} %bitcast.5, f32[1,16]{1,0:T(1,128)} %bitcast.6, f32[1,128]{1,0:T(1,128)} %bitcast.7), custom_call_target="tpu_custom_call" | custom-call | flops 2000000000 | bytes 8000000 | tf_op jit(solution)/shard_map/ladder_cycle/pallas_call | solution.py:419
  44.0 0.6 %copy.7 = f32[1,128,128]{2,1,0:T(8,128)} copy(f32[1,128,128]{2,1,0:T(8,128)S(1)} %bitcast.4) | data formatting | bytes 131072

commit v6 on v5

--- a/solution.py
+++ b/solution.py
@@ -103,7 +103,7 @@
 
     def remote(n, src, dst, device):
         c = pltpu.make_async_remote_copy(
-            src_ref=src, dst_ref=dst, send_sem=ssem.at[n], recv_sem=rsem.at[n],
+            src_ref=src, dst_ref=dst, send_sem=ssem.at[len(sends)], recv_sem=rsem.at[n],
             device_id=device, device_id_type=pl.DeviceIdType.MESH,
         )
         c.start()
@@ -111,7 +111,7 @@
 
     def arrive(n, dst):
         pltpu.make_async_remote_copy(
-            src_ref=dst, dst_ref=dst, send_sem=ssem.at[n], recv_sem=rsem.at[n],
+            src_ref=dst, dst_ref=dst, send_sem=ssem.at[0], recv_sem=rsem.at[n],
             device_id=sib, device_id_type=pl.DeviceIdType.MESH,
         ).wait_recv()
 
@@ -152,21 +152,19 @@
 
         if k == 0:
             for dy in range(1, NY):
-                remote(sem((q, "y", dy)), gat.at[y, z], gat.at[y, z], dev(at_y(dy), z, h, x))
+                remote(sem((q, "y")), gat.at[y, z], gat.at[y, z], dev(at_y(dy), z, h, x))
             return
         if k == 1:
-            for dy in range(1, NY):
-                arrive(sem((q, "y", dy)), gat.at[at_y(-dy), z])
+            arrive(sem((q, "y")), gat.at[0:3, z])
         for p in pieces:
             if k > 1:
-                for sign in (1, -1):
-                    if last(p, sign, k - 1):
-                        arrive(sem((q, "z", k - 1, sign, p)), group(p, -sign * (k - 1)))
+                both = gat.at[:, z] if k < 5 else group(p, 4)
+                arrive(sem((q, "z", k - 1, p)), both)
             if k < 5:
                 for sign in (1, -1):
                     if last(p, sign, k):
                         b = group(p, -sign * (k - 1))
-                        remote(sem((q, "z", k, sign, p)), b, b, dev(y, at_z(sign), h, x))
+                        remote(sem((q, "z", k, p)), b, b, dev(y, at_z(sign), h, x))
 
     def zy(q, k):
         gat = gats[q]
@@ -175,53 +173,45 @@
         cut = {1: pl.ds(0, half), -1: pl.ds(half, rows - half)}
 
         def own_z(d):
-            remote(sem((q, "z", d)), gat.at[y, z], gat.at[y, z], dev(y, at_z(d), h, x))
+            remote(sem((q, "z", abs(d))), gat.at[y, z], gat.at[y, z], dev(y, at_z(d), h, x))
 
         def got_z(d):
-            if abs(d) < 4:
-                arrive(sem((q, "z", -d)), gat.at[y, at_z(d)])
-            else:
-                for sign in (1, -1):
-                    arrive(sem((q, "z4", sign)), gat.at[y, at_z(4), cut[sign]])
+            arrive(sem((q, "z", d)), gat.at[0:2, z] if d < 4 else gat.at[y, at_z(4)])
 
         def forward_z(sign):
             b = gat.at[y, at_z(-2 * sign)]
-            remote(sem((q, "z", 3 * sign)), b, b, dev(y, at_z(sign), h, x))
+            remote(sem((q, "z", 3)), b, b, dev(y, at_z(sign), h, x))
             c = gat.at[y, at_z(-2 * sign), cut[sign]]
-            remote(sem((q, "z4", sign)), c, c, dev(y, at_z(2 * sign), h, x))
+            remote(sem((q, "z", 4)), c, c, dev(y, at_z(2 * sign), h, x))
 
         def y1(d):
             for sign in (1, -1):
                 b = gat.at[y, at_z(d)]
-                remote(sem((q, "y1", d, sign)), b, b, dev(at_y(sign), z, h, x))
+                remote(sem((q, "y1", d)), b, b, dev(at_y(sign), z, h, x))
 
         def got_y1(d):
-            for sign in (1, -1):
-                arrive(sem((q, "y1", d, sign)), gat.at[at_y(-sign), at_z(d)])
+            arrive(sem((q, "y1", d)), gat.at[0:2, z])
 
         def y2(d, sign):
             b = gat.at[at_y(-sign), at_z(d)]
-            remote(sem((q, "y2", d)), b, b, dev(at_y(sign), z, h, x))
-
-        def got_y2(d):
-            arrive(sem((q, "y2", d)), gat.at[at_y(2), at_z(d)])
+            remote(sem((q, "y2")), b, b, dev(at_y(sign), z, h, x))
 
         if k == 0:
             for d in (1, -1, 2, -2):
                 own_z(d)
             y1(0)
         elif k == 1:
-            got_z(1); got_z(-1)
+            got_z(1)
             y1(1); y1(-1)
         elif k == 2:
-            got_z(2); got_z(-2)
+            got_z(2)
             forward_z(1); forward_z(-1)
             y1(2); y1(-2)
         elif k == 3:
             got_y1(0)
             y2(0, 1)
         elif k == 4:
-            got_z(3); got_z(-3)
+            got_z(3)
             y1(3); y1(-3)
         elif k == 5:
             got_y1(1); got_y1(-1)
@@ -239,8 +229,7 @@
             got_y1(4)
             y2(4, -1)
         elif k == 10:
-            for d in (0, 1, -1, -2, 2, 3, -3, 4):
-                got_y2(d)
+            arrive(sem((q, "y2")), gat.at[at_y(2)])
 
     def prepare_ints(q):
         vcopies[q].wait()
@@ -393,7 +382,8 @@
         a2a(k, (u + k) % 32, u).start()
         return carry
 
-    lax.fori_loop(1, 32, a2a_start, 0)
+    for k in range(1, 32):
+        a2a_start(k, 0)
     keep = pltpu.make_async_copy(fin.at[pl.ds(place(u), 4), :], land.at[pl.ds(u * 4, 4), :], lsem.at[6])
     keep.start()
     keep.wait()

time: 44.7 us -> 44.6 us (level)
  no operation moved by 1% of the time
where the time goes in v6:
time: 44.6 us; the launch traced here: 44.5 us
  Pallas kernels  43.9 us (98%)
  local copies, waits for them, and re-layouts  0.63 us (1%)
    pallas_call x1, Pallas kernels, body(): pl.pallas_call(kernel, out_shape=pltpu.VMEM((128, 128), F32), in_specs=[p...  43.9 us

profile of v6, /device:TPU:1, one launch (start us, length us, event | category | flops | bytes accessed | tf_op | source)
XLA Modules:
  0.0 44.5 jit_solution(1710278364185298193)
XLA Ops:
  0.0 43.9 %ladder_cycle.1 = f32[128,128]{1,0:T(8,128)S(1)} custom-call(f32[4,32,128]{2,1,0:T(8,128)} %amps.1, f32[32,128,256]{2,1,0:T(8,128)} %ints.1, f32[16,16,32,128]{3,2,1,0:T(8,128)} %bitcast.5, f32[1,16]{1,0:T(1,128)} %bitcast.6, f32[1,128]{1,0:T(1,128)} %bitcast.7), custom_call_target="tpu_custom_call" | custom-call | flops 2000000000 | bytes 8000000 | tf_op jit(solution)/shard_map/ladder_cycle/pallas_call | solution.py:409
  43.9 0.6 %copy.7 = f32[1,128,128]{2,1,0:T(8,128)} copy(f32[1,128,128]{2,1,0:T(8,128)S(1)} %bitcast.4) | data formatting | bytes 131072
